TPU v7x, 512 devices: a whole 4x4x16 slice. The times are simulated.
512 devices in a mesh: row: 16 (over y_lo, x, core), col: 32 (over y_hi, z).
Axes of the slice: x: 4, y: 4 (y_hi: 2, y_lo: 2; y = y_hi * 2 + y_lo), z: 16, core: 2. Of those that a mesh axis runs over, the one named last changes fastest.
Arguments:
- p_blocks: bfloat16 [1024, 128, 256], P(('row', 'col')), may hold values from -0.5 to 0.5
- a_blocks: bfloat16 [1024, 4096, 128], P('row', 'col'), may hold values from -6 to 6
- a_owner: int32 [16, 512], P('row', 'col'), may hold values from 0 to 31
- a_row: int32 [512, 64], P('row', 'col'), may hold values from 0 to 1
- a_count: int32 [256, 64], P('row', 'col'), may hold values from 0 to 2, as said below
Outputs:
- coarse_op: bfloat16 [256, 8192, 256], P('row', 'col')
Inputs may be any that keep to these rules, and one draw needn't show every extreme that they name: `a_count`: live blocks of one bucket are at most 2, and 2 is reached in every draw; the live load differs from tile to tile.
All inputs are finite; a program needn't handle non-finite values.
Results may differ from a plain program's by a relative error of at most 0.0049.
Values may be sent and summed in bfloat16 or wider, within the bound.
No kernel may reach another device: no remote copies, remote signals or barrier semaphores. Data moves between devices by JAX's collectives and lax.ppermute only.
A program may use at most 64 MiB of HBM per device.

v0:
```python
import jax
import jax.numpy as jnp
from jax import lax
from jax.sharding import PartitionSpec as P


def on_device(p_blocks, a_blocks, a_owner, a_row, a_count):
    groups = lax.axis_size("row")
    fine_count = p_blocks.shape[0]
    block_size = p_blocks.shape[1]
    coarse_width = p_blocks.shape[2]
    capacity = a_row.shape[1]
    panels = lax.all_gather(p_blocks, "col", axis=0, tiled=True)
    picked = a_owner.reshape(groups, 1, 1) * fine_count + a_row.reshape(
        groups, fine_count, capacity
    )
    chosen = jnp.take(panels, picked, axis=0)
    tile_blocks = a_blocks.reshape(groups, fine_count, capacity, block_size, block_size)
    slot_terms = lax.dot_general(
        tile_blocks,
        chosen,
        (((3,), (3,)), ((0, 1, 2), (0, 1, 2))),
        preferred_element_type=jnp.float32,
    )
    is_live = jnp.arange(capacity, dtype=jnp.int32)[None, None, :] < a_count[:, :, None]
    slot_terms = jnp.where(is_live[..., None, None], slot_terms, 0.0).astype(jnp.bfloat16)
    arrived = lax.all_to_all(slot_terms, "row", split_axis=0, concat_axis=0, tiled=True)
    spread = jnp.broadcast_to(
        p_blocks.reshape(fine_count, 1, block_size, coarse_width),
        (fine_count, capacity, block_size, coarse_width),
    )
    result = lax.dot_general(
        arrived, spread, (((1, 2, 3), (0, 1, 2)), ((), ())), preferred_element_type=jnp.float32
    )
    return result.astype(jnp.bfloat16)


def solution(mesh):
    in_specs = (
        P(("row", "col"), None, None),
        P("row", "col", None),
        P("row", "col"),
        P("row", "col"),
        P("row", "col"),
    )
    out_specs = P("row", "col", None)
    return jax.shard_map(
        on_device, mesh=mesh, in_specs=in_specs, out_specs=out_specs, check_vma=False
    )
```

profile of v0, /device:TPU:1, one launch (start us, length us, event | category | flops | bytes accessed | tf_op | source)
XLA Modules:
  0.0 258.3 jit_solution(17478261765161315398)
XLA Ops:
  6.5 0.0 copy-start
  6.5 0.0 all-gather.2.cloned.1.call-start
  6.5 0.7 all-gather.2.cloned.1.call-update
  7.3 0.8 reshape.50
  8.0 0.8 reshape.49
  8.8 0.8 copy.17
  9.6 0.7 multiply_bitcast_fusion
  10.2 0.1 compare_select_fusion
  10.3 0.2 copy.20
  10.5 0.1 reshape.54
  10.6 0.1 copy.18
  10.7 0.1 copy.19
  10.8 0.1 iota_compare_fusion
  10.9 161.0 %all-gather.2.cloned.1.call-done = bf16[64,128,256]{2,1,0:T(8,128)(2,1)} async-done(((bf16[2,128,256]{2,1,0:T(8,128)(2,1)}), bf16[64,128,256]{2,1,0:T(8,128)(2,1)}) %all-gather.2.cloned.1.call-update) | async-done | bytes 4194320 | tf_op jit(solution)/shard_map/all_gather | solution.py:13
  171.9 4.9 %gather_fusion = bf16[64,128,256]{2,1,0:T(8,128)(2,1)} fusion(bf16[64,128,256]{2,1,0:T(8,128)(2,1)} %all-gather.2.cloned.1.call-done, s32[1024]{0:T(1024)S(1)} %pad_clamp_fusion), kind=kCustom, calls=%fused_computation | custom fusion | bytes 8388864 | tf_op jit(solution)/shard_map/jit(_take)/gather | solution.py:17
  176.8 6.4 %copy.21 = bf16[16,2,2,128,256]{3,4,2,1,0:T(8,128)(2,1)} copy(bf16[16,2,2,128,256]{4,3,2,1,0:T(8,128)(2,1)} %bitcast.24) | data formatting | bytes 8388608 | tf_op jit(solution)/shard_map/jit(_take)/gather | solution.py:17
  183.3 0.0 copy-done
  183.3 3.5 %fusion = bf16[16,2,2,128,256]{3,4,2,1,0:T(8,128)(2,1)S(1)} fusion(pred[16,2,2]{2,1,0:T(4,128)(4,1)S(1)} %iota_compare_fusion, bf16[16,2,2,128,128]{4,3,2,1,0:T(8,128)(2,1)S(1)} %bitcast.23, bf16[16,2,2,128,256]{3,4,2,1,0:T(8,128)(2,1)} %copy.21, pred[16,2,2]{2,1,0:T(4,128)(4,1)S(1)} %copy.19), kind=kOutput, calls=%fused_computation.2 | convolution fusion | flops 543162368 | bytes 10485888 | tf_op jit(solution)/shard_map/dot_general | solution.py:19
  186.8 0.0 copy-start.1
  186.8 62.1 %all_to_all.5 = bf16[16,2,2,128,256]{3,4,2,1,0:T(8,128)(2,1)S(1)} all-to-all(bf16[16,2,2,128,256]{3,4,2,1,0:T(8,128)(2,1)S(1)} %fusion), channel_id=1, replica_groups=mesh['row'=16,'col'=32] {'row'}, dimensions={0} | all-to-all | bytes 8388608 | tf_op jit(solution)/shard_map/all_to_all | solution.py:27
  248.9 0.0 copy-done.1
  248.9 2.6 bitcast_convert_fusion
  (2 shorter events, 0.0 us)
Async XLA Ops:
  6.5 176.7 %copy-start = (bf16[64,128,128]{2,1,0:T(8,128)(2,1)S(1)}, bf16[64,128,128]{2,1,0:T(8,128)(2,1)}, u32[]{:S(2)}) copy-start(bf16[64,128,128]{2,1,0:T(8,128)(2,1)} %param.6) | copy-start | bytes 6291460
  6.5 165.4 %all-gather.2.cloned.1.call-start = ((), (), s32[]{:S(2)}) async-start(), calls=%async_computation.1 | async-start | bytes 4325376 | tf_op jit(solution)/shard_map/all_gather | solution.py:13
  186.8 62.1 %copy-start.1 = (bf16[2,128,256]{2,1,0:T(8,128)(2,1)S(1)}, bf16[2,128,256]{2,1,0:T(8,128)(2,1)}, u32[]{:S(2)}) copy-start(bf16[2,128,256]{2,1,0:T(8,128)(2,1)} %param.5) | copy-start | bytes 393220
Sparse Core Ops, SparseCore 0:
  10.5 161.3 all-gather.1
where the time goes:
time: 259 us; the launch traced here: 258 us
  waiting for transfers between devices  162 us (63%)
  blocking collectives  62.1 us (24%)
  local copies, waits for them, and re-layouts  14.2 us (5%)
  between operations  13.4 us (5%)
  matrix products  6.07 us (2%)
    all_gather x1, waiting for transfers between devices, on_device(): panels = lax.all_gather(p_blocks, 'col', axis=0, tiled=True)  161 us
    all_to_all x1, blocking collectives, on_device(): lax.all_to_all(slot_terms, 'row', split_axis=0, concat_axis=0, tiled=True)  62.1 us
    gather x2, local copies, waits for them, and re-layouts, on_device(): chosen = jnp.take(panels, picked, axis=0)  11.4 us
  transfers between devices with their start and end apart: 1, of which 1 were waited for; matrix products, arithmetic and copies ran while one was open for 1% of the time, Pallas kernels for 0%

commit v1 on v0

--- a/solution.py
+++ b/solution.py
@@ -10,7 +10,9 @@
     block_size = p_blocks.shape[1]
     coarse_width = p_blocks.shape[2]
     capacity = a_row.shape[1]
-    panels = lax.all_gather(p_blocks, "col", axis=0, tiled=True)
+    panels = jnp.concatenate(
+        lax.all_to_all(jnp.stack([p_blocks] * lax.axis_size("col")), "col", 0, 0), axis=0
+    )
     picked = a_owner.reshape(groups, 1, 1) * fine_count + a_row.reshape(
         groups, fine_count, capacity
     )

time: 259 us -> 285 us (1.10); the launches traced: 258 us -> 281 us
  waiting for transfers between devices: 162 us -> 185 us
  starting transfers between devices: 0.01 us -> 18.9 us
  between operations: 13.4 us -> 0.08 us
  blocking collectives: 62.1 us -> 55.2 us
    all_to_all x0 -> x1, waiting for transfers between devices: none -> 185 us  [on_device(): lax.all_to_all(jnp.stack([p_blocks] * lax.axis_size('col')), 'col', 0, 0)]
    all_gather x1 -> x0, waiting for transfers between devices: 161 us -> none  [on_device(): panels = lax.all_gather(p_blocks, 'col', axis=0, tiled=True)]
    all_to_all x0 -> x1, starting transfers between devices: none -> 18.9 us  [on_device(): lax.all_to_all(jnp.stack([p_blocks] * lax.axis_size('col')), 'col', 0, 0)]
    all_to_all x1, blocking collectives: 62.1 us -> 55.2 us  [on_device(): lax.all_to_all(slot_terms, 'row', split_axis=0, concat_axis=0, tiled=True)]
    another operation x0 -> x1, local copies, waits for them, and re-layouts: none -> 3.53 us  [on_device(): jnp.stack([p_blocks] * lax.axis_size('col'))]
  transfers between devices with their start and end apart: 1 -> 1, of which waited for: 1 -> 1; matrix products, arithmetic and copies ran while one was open for 1% -> 0% of each run, Pallas kernels for 0% -> 0%
where the time goes in v1:
time: 285 us; the launch traced here: 281 us
  waiting for transfers between devices  185 us (65%)
  blocking collectives  55.2 us (19%)
  starting transfers between devices  18.9 us (7%)
  local copies, waits for them, and re-layouts  15.7 us (6%)
  matrix products  6.07 us (2%)
    all_to_all x1, waiting for transfers between devices, on_device(): lax.all_to_all(jnp.stack([p_blocks] * lax.axis_size('col')), 'col', 0, 0)  185 us
    all_to_all x1, blocking collectives, on_device(): lax.all_to_all(slot_terms, 'row', split_axis=0, concat_axis=0, tiled=True)  55.2 us
    all_to_all x1, starting transfers between devices, on_device(): lax.all_to_all(jnp.stack([p_blocks] * lax.axis_size('col')), 'col', 0, 0)  18.9 us
    gather x2, local copies, waits for them, and re-layouts, on_device(): chosen = jnp.take(panels, picked, axis=0)  11.4 us
  transfers between devices with their start and end apart: 1, of which 1 were waited for; matrix products, arithmetic and copies ran while one was open for 0% of the time, Pallas kernels for 0%

profile of v1, /device:TPU:1, one launch (start us, length us, event | category | flops | bytes accessed | tf_op | source)
XLA Modules:
  0.0 280.6 jit_solution(15193298624204147795)
XLA Ops:
  0.0 0.0 copy-start
  0.0 3.5 %stack.2 = bf16[32,2,128,256]{3,2,1,0:T(8,128)(2,1)} broadcast(bf16[2,128,256]{2,1,0:T(8,128)(2,1)} %param.5), dimensions={1,2,3} | broadcast | bytes 4325376 | tf_op jit(solution)/shard_map/stack | solution.py:14
  3.5 18.9 %all-to-all-start = ((bf16[32,2,128,256]{3,2,1,0:T(8,128)(2,1)}), bf16[32,2,128,256]{3,2,1,0:T(8,128)(2,1)}, u32[]{:S(2)}, u32[]{:S(2)}) async-start(bf16[32,2,128,256]{3,2,1,0:T(8,128)(2,1)} %stack.2), calls=%async_computation | async-start | bytes 8388608 | tf_op jit(solution)/shard_map/all_to_all | solution.py:14
  22.5 0.0 copy-done.2
  22.5 0.1 reshape.56
  22.6 0.1 reshape.54
  22.6 0.0 copy-done.4
  22.7 0.1 compare_select_fusion
  22.7 0.2 copy.20
  23.0 0.1 reshape.60
  23.1 0.1 copy.18
  23.2 0.1 copy.19
  23.3 0.0 copy-done.3
  23.3 0.1 copy.17
  23.4 0.1 iota_compare_fusion
  23.5 184.5 %all-to-all-done = bf16[32,2,128,256]{3,2,1,0:T(8,128)(2,1)} async-done(((bf16[32,2,128,256]{3,2,1,0:T(8,128)(2,1)}), bf16[32,2,128,256]{3,2,1,0:T(8,128)(2,1)}, u32[]{:S(2)}, u32[]{:S(2)}) %all-to-all-start) | async-done | bytes 4194336 | tf_op jit(solution)/shard_map/all_to_all | solution.py:14
  208.0 5.0 %gather_fusion = bf16[64,128,256]{2,1,0:T(8,128)(2,1)} fusion(bf16[64,128,256]{2,1,0:T(8,128)(2,1)} %bitcast.1, s32[1024]{0:T(1024)S(1)} %pad_clamp_fusion), kind=kCustom, calls=%fused_computation | custom fusion | bytes 8388864 | tf_op jit(solution)/shard_map/jit(_take)/gather | solution.py:19
  213.0 6.4 %copy.21 = bf16[16,2,2,128,256]{3,4,2,1,0:T(8,128)(2,1)} copy(bf16[16,2,2,128,256]{4,3,2,1,0:T(8,128)(2,1)} %bitcast.25) | data formatting | bytes 8388608 | tf_op jit(solution)/shard_map/jit(_take)/gather | solution.py:19
  219.3 0.0 copy-done
  219.3 3.5 %fusion = bf16[16,2,2,128,256]{3,4,2,1,0:T(8,128)(2,1)S(1)} fusion(pred[16,2,2]{2,1,0:T(4,128)(4,1)S(1)} %iota_compare_fusion, bf16[16,2,2,128,128]{4,3,2,1,0:T(8,128)(2,1)S(1)} %bitcast.24, bf16[16,2,2,128,256]{3,4,2,1,0:T(8,128)(2,1)} %copy.21, pred[16,2,2]{2,1,0:T(4,128)(4,1)S(1)} %copy.19), kind=kOutput, calls=%fused_computation.2 | convolution fusion | flops 543162368 | bytes 10485888 | tf_op jit(solution)/shard_map/dot_general | solution.py:21
  222.9 0.0 copy-start.1
  222.9 55.2 %all_to_all.10 = bf16[16,2,2,128,256]{3,4,2,1,0:T(8,128)(2,1)S(1)} all-to-all(bf16[16,2,2,128,256]{3,4,2,1,0:T(8,128)(2,1)S(1)} %fusion), channel_id=1, replica_groups=mesh['row'=16,'col'=32] {'row'}, dimensions={0} | all-to-all | bytes 8388608 | tf_op jit(solution)/shard_map/all_to_all | solution.py:29
  278.0 0.0 copy-done.1
  278.0 2.6 bitcast_convert_fusion
  (6 shorter events, 0.0 us)
Async XLA Ops:
  0.0 219.3 %copy-start = (bf16[64,128,128]{2,1,0:T(8,128)(2,1)S(1)}, bf16[64,128,128]{2,1,0:T(8,128)(2,1)}, u32[]{:S(2)}) copy-start(bf16[64,128,128]{2,1,0:T(8,128)(2,1)} %param.6) | copy-start | bytes 6291460
  3.5 18.9 %copy-start.2 = (s32[32,2]{0,1:T(2,128)S(1)}, s32[32,2]{0,1:T(2,128)}, u32[]{:S(2)}) copy-start(s32[32,2]{0,1:T(2,128)} %param.8) | copy-start | bytes 772
  3.5 19.1 %copy-start.4 = (s32[1,16]{1,0:T(1,128)S(1)}, s32[1,16]{1,0:T(1,128)}, u32[]{:S(2)}) copy-start(s32[1,16]{1,0:T(1,128)} %param.7) | copy-start | bytes 196
  3.5 19.8 %copy-start.3 = (s32[16,2]{0,1:T(2,128)S(1)}, s32[16,2]{0,1:T(2,128)}, u32[]{:S(2)}) copy-start(s32[16,2]{0,1:T(2,128)} %param.9) | copy-start | bytes 388
  3.5 204.4 %all-to-all-start = ((bf16[32,2,128,256]{3,2,1,0:T(8,128)(2,1)}), bf16[32,2,128,256]{3,2,1,0:T(8,128)(2,1)}, u32[]{:S(2)}, u32[]{:S(2)}) async-start(bf16[32,2,128,256]{3,2,1,0:T(8,128)(2,1)} %stack.2), calls=%async_computation | async-start | bytes 8388608 | tf_op jit(solution)/shard_map/all_to_all | solution.py:14
  222.9 55.2 %copy-start.1 = (bf16[2,128,256]{2,1,0:T(8,128)(2,1)S(1)}, bf16[2,128,256]{2,1,0:T(8,128)(2,1)}, u32[]{:S(2)}) copy-start(bf16[2,128,256]{2,1,0:T(8,128)(2,1)} %param.5) | copy-start | bytes 393220
